TPU v7x, 32 devices: a whole 2x2x4 slice. The times are simulated.
32 devices in a mesh: ctx: 16 (over z, y, x), dp: 2 (over core).
Axes of the slice: x: 2, y: 2, z: 4, core: 2. Of those that a mesh axis runs over, the one named last changes fastest.
Arguments:
- query_rows: bfloat16 [8192, 1024], P(('dp', 'ctx')), parts along dimension 0, may hold values from -100 to 100
- key_rows: bfloat16 [8192, 1024], P(('dp', 'ctx')), parts along dimension 0, may hold values from -5 to 5
- value_rows: bfloat16 [8192, 1024], P(('dp', 'ctx')), parts along dimension 0, may hold values from -6 to 6
- channels: bfloat16 [8192, 2048], P(('dp', 'ctx')), parts along dimension 0, may hold values from -6 to 6
- step_low: bfloat16 [8192, 128], P(('dp', 'ctx')), parts along dimension 0, may hold values from -6 to 6
- step_proj: bfloat16 [128, 2048], replicated, may hold values from -0.5 to 0.5
- step_bias: float32 [2048], replicated, may hold values from -8 to -2.5
- decay_log: float32 [16, 2048], replicated, may hold values from -6.5 to -0.5
- state_maps: float32 [2, 16, 8192], P(None, None, ('dp', 'ctx')), parts along dimension 2, may hold values from -6 to 6
- attend_weight: bfloat16 [1024, 128], replicated, may hold values from -0.5 to 0.5
- mixer_weight: bfloat16 [2048, 128], replicated, may hold values from -0.125 to 0.125
Outputs:
- token_vectors: bfloat16 [8192, 128], P(('dp', 'ctx')), parts along dimension 0
There are 2 independent parts, one for each index of `dp`. A program takes and returns all parts, laid end to end along the dimension named above; an argument that names none is the same for every part. Nothing has to cross between parts.
All inputs are finite; a program needn't handle non-finite values.
Results may differ from a plain program's by a relative error of at most 0.005.
Values may be sent and summed in bfloat16 or wider, within the bound.
A program may use at most 128 MiB of HBM per device.

v0:
```python
import math

import jax
import jax.numpy as jnp
from jax import lax
from jax.sharding import PartitionSpec as P

HD = 128


def entering_2(part, axis, combine, identity):
    place = lax.axis_index(axis)
    gathered = jax.tree.map(lambda a: lax.all_gather(a, axis), part)
    state = jax.tree.map(lambda a, e: jnp.zeros_like(a) + jnp.asarray(e, a.dtype), part, identity)

    def one(hop, state):
        return combine(
            state, jax.tree.map(lambda a: lax.dynamic_index_in_dim(a, hop, 0, False), gathered)
        )

    return lax.fori_loop(0, place, one, state)


def from_behind(value, axis, steps):
    count = lax.axis_size(axis)
    initial, last = (max(0, -steps), min(count, count - steps))
    return lax.ppermute(value, axis, [(source, source + steps) for source in range(initial, last)])


def attention(query_rows, window, position):
    shard_rows, feature_count = query_rows.shape
    head_count = feature_count // HD
    window_rows = 4 * shard_rows
    query_block = query_rows.reshape(shard_rows, head_count, HD)
    key_block = window[0].reshape(5 * shard_rows, head_count, HD)
    value_block = window[1].reshape(5 * shard_rows, head_count, HD)
    scores = jnp.einsum(
        "qhd,khd->hqk", query_block, key_block, preferred_element_type=jnp.float32
    ) * (1.0 / math.sqrt(HD))
    query_pos = jnp.arange(shard_rows, dtype=jnp.int32)[:, None]
    column = jnp.arange(5 * shard_rows, dtype=jnp.int32)[None, :]
    offset = column - window_rows
    allowed = (
        (offset <= query_pos)
        & (query_pos - offset < window_rows)
        & (position * shard_rows + offset >= 0)
    )
    scores = jnp.where(allowed[None], scores, -1e30)
    row_max = jnp.max(scores, -1, keepdims=True)
    exp_terms = jnp.exp(scores - row_max)
    row_sum = jnp.sum(exp_terms, -1)
    weights = exp_terms.astype(jnp.bfloat16)
    summed = jnp.einsum("hqk,khd->qhd", weights, value_block, preferred_element_type=jnp.float32)
    result = summed / jnp.transpose(row_sum)[:, :, None]
    return result.reshape(shard_rows, feature_count).astype(jnp.bfloat16)


def run_mixer(carry_state, timestep, inflow, in_maps, out_maps, decay_rate):
    shard_rows = timestep.shape[0]
    block_len = math.gcd(16, shard_rows)
    groups = shard_rows // block_len

    def advance(running, inputs):
        step_blk, inflow_blk, in_blk, out_blk = inputs
        collected = []
        for offset in range(block_len):
            running = (
                jnp.exp(step_blk[offset][None, :] * decay_rate) * running
                + in_blk[offset][:, None] * inflow_blk[offset][None, :]
            )
            collected.append(jnp.sum(out_blk[offset][:, None] * running, 0))
        return (running, jnp.stack(collected))

    final_state, outputs = lax.scan(
        advance,
        carry_state,
        (
            timestep.reshape(groups, block_len, -1),
            inflow.reshape(groups, block_len, -1),
            in_maps.reshape(groups, block_len, -1),
            out_maps.reshape(groups, block_len, -1),
        ),
    )
    return (final_state, outputs.reshape(shard_rows, -1))


def combine(earlier, following):
    return (earlier[0] * following[0], following[0] * earlier[1] + following[1])


def prefix_state(through, local_end):
    identity = (jnp.ones_like(through), jnp.zeros_like(local_end))
    result = entering_2((through, local_end), "ctx", combine, identity)
    return result[1]


def per_device(
    query_rows,
    key_rows,
    value_rows,
    channels,
    step_low,
    step_proj,
    step_bias,
    decay_log,
    state_maps,
    attend_weight,
    mixer_weight,
):
    position = lax.axis_index("ctx")
    stacked = jnp.stack([key_rows, value_rows])
    earlier = []
    moving = stacked
    for distance in range(1, 5):
        moving = from_behind(moving, "ctx", 1)
        earlier.append(moving)
    window = jnp.concatenate(earlier[::-1] + [stacked], 1)
    attended = attention(query_rows, window, position)
    timestep = jax.nn.softplus(
        jnp.dot(step_low, step_proj, preferred_element_type=jnp.float32) + step_bias
    )
    decay_rate = -jnp.exp(decay_log)
    inflow = timestep * channels.astype(jnp.float32)
    in_maps = jnp.transpose(state_maps[0])
    out_maps = jnp.transpose(state_maps[1])
    zero_state = jnp.zeros(decay_log.shape, jnp.float32)
    shard_rows = timestep.shape[0]
    lower_ones = (jnp.arange(shard_rows)[:, None] >= jnp.arange(shard_rows)[None, :]).astype(
        jnp.float32
    )
    cumulative = jnp.dot(lower_ones, timestep, precision=lax.Precision.HIGHEST)
    local_end, outputs = run_mixer(zero_state, timestep, inflow, in_maps, out_maps, decay_rate)
    through = jnp.exp(decay_rate * cumulative[-1][None, :])
    entering = prefix_state(through, local_end)
    for state_index in range(decay_rate.shape[0]):
        outputs = (
            outputs
            + out_maps[:, state_index][:, None]
            * jnp.exp(cumulative * decay_rate[state_index][None, :])
            * entering[state_index][None, :]
        )
    mixer_norm = (
        outputs * lax.rsqrt(jnp.mean(outputs * outputs, -1, keepdims=True) + 1e-05)
    ).astype(jnp.bfloat16)
    combined = jnp.dot(attended, attend_weight, preferred_element_type=jnp.float32) + jnp.dot(
        mixer_norm, mixer_weight, preferred_element_type=jnp.float32
    )
    return (combined * lax.rsqrt(jnp.mean(combined * combined, -1, keepdims=True) + 1e-06)).astype(
        jnp.bfloat16
    )


def solution(mesh):
    return jax.shard_map(
        per_device,
        mesh=mesh,
        in_specs=(
            P(("dp", "ctx"), None),
            P(("dp", "ctx"), None),
            P(("dp", "ctx"), None),
            P(("dp", "ctx"), None),
            P(("dp", "ctx"), None),
            P(),
            P(),
            P(),
            P(None, None, ("dp", "ctx")),
            P(),
            P(),
        ),
        out_specs=P(("dp", "ctx"), None),
        check_vma=False,
    )
```

profile of v0, /device:TPU:24, one launch (start us, length us, event | category | flops | bytes accessed | tf_op | source)
XLA Modules:
  0.0 230.9 jit_solution(18438824675683776728)
XLA Ops:
  6.5 4.3 %convert_multiply_fusion = (f32[256,2048]{1,0:T(8,128)}, f32[256,2048]{1,0:T(8,128)S(1)}) fusion(bf16[256,2048]{1,0:T(8,128)(2,1)} %param.18, f32[2048]{0:T(1024)} %param.21, bf16[256,128]{1,0:T(8,128)(2,1)} %param.19, bf16[128,2048]{1,0:T(8,128)(2,1)} %param.20), kind=kOutput, calls=%fused_computation.159 | convolution fusion | flops 138936320 | bytes 5840896 | tf_op jit(solution)/shard_map/dot_general | solution.py:120
  10.8 1.2 fusion.66
  12.1 1.3 copy-done.2
  13.4 0.7 exponential_negate_fusion
  14.8 69.0 %while.26 = (s32[]{:T(128)}, f32[16,2048]{1,0:T(8,128)S(1)}, f32[16,16,2048]{2,1,0:T(8,128)}, f32[16,16,2048]{2,1,0:T(8,128)S(1)}, f32[16,2048]{1,0:T(8,128)S(1)...) while((s32[]{:T(128)}, f32[16,2048]{1,0:T(8,128)S(1)}, ...), condition=%wide.region_19.20_spmd.clone, body=%wide.region_2.19_spmd.clone.sunk | while | flops 4620306 | bytes 3988712 | solution.py:74
  14.9 1.9 constant_dynamic-slice_fusion.65
  18.4 0.7 bitcast_dynamic-update-slice_fusion.2
  19.1 2.1 constant_dynamic-slice_fusion.65
  22.8 0.7 bitcast_dynamic-update-slice_fusion.2
  23.5 1.9 constant_dynamic-slice_fusion.65
  27.0 0.7 bitcast_dynamic-update-slice_fusion.2
  27.7 1.9 constant_dynamic-slice_fusion.65
  31.2 0.7 bitcast_dynamic-update-slice_fusion.2
  31.9 1.9 constant_dynamic-slice_fusion.65
  35.4 0.7 bitcast_dynamic-update-slice_fusion.2
  36.1 1.9 constant_dynamic-slice_fusion.65
  39.6 0.7 bitcast_dynamic-update-slice_fusion.2
  40.3 2.2 constant_dynamic-slice_fusion.65
  44.8 2.4 %constant_dynamic-slice_fusion.65 = (f32[1,1,2048]{2,1,0:T(1,128)S(1)}, f32[1,1,2048]{2,1,0:T(1,128)S(1)}, f32[1,1,2048]{2,1,0:T(1,128)S(1)}, f32[1,1,2048]{2,1,...) fusion(f32[16,16,2048]{2,1,0:T(8,128)} %get-tuple-element.634, ...), kind=kLoop, calls=%fused_computation.79.clone.1 | loop fusion | bytes 524352 | tf_op jit(solution)/shard_map/while/body/eval_jaxpr/slice | solution.py:69
  48.8 0.7 bitcast_dynamic-update-slice_fusion.2
  49.5 1.9 constant_dynamic-slice_fusion.65
  53.0 0.7 bitcast_dynamic-update-slice_fusion.2
  53.7 1.9 constant_dynamic-slice_fusion.65
  57.2 0.7 bitcast_dynamic-update-slice_fusion.2
  57.9 1.9 constant_dynamic-slice_fusion.65
  61.4 0.7 bitcast_dynamic-update-slice_fusion.2
  62.1 2.2 constant_dynamic-slice_fusion.65
  66.5 1.9 constant_dynamic-slice_fusion.65
  70.7 2.2 constant_dynamic-slice_fusion.65
  74.5 0.7 bitcast_dynamic-update-slice_fusion.2
  75.2 1.9 constant_dynamic-slice_fusion.65
  79.4 2.2 constant_dynamic-slice_fusion.65
  83.1 0.7 bitcast_dynamic-update-slice_fusion.2
  84.5 1.2 copy.19
  85.8 1.2 copy.18
  87.1 3.4 %collective-permute-start = (bf16[2,256,1024]{1,2,0:T(8,128)(2,1)S(1)}, bf16[2,256,1024]{1,2,0:T(8,128)(2,1)S(1)}, u32[]{:S(2)}, u32[]{:S(2)}) collective-permute-start(bf16[2,256,1024]{1,2,0:T(8,128)(2,1)S(1)} %pad_maximum_fusion), channel_id=1, source_target_pairs={{0,2},{2,4},{4,6},{6,8},{8,10},{10,12},{12,14},{14,16},{16,18},{18... | collective-permute-start | bytes 3145736 | tf_op jit(solution)/shard_map/ppermute | solution.py:27
  90.5 31.7 %collective-permute-done = bf16[2,256,1024]{1,2,0:T(8,128)(2,1)S(1)} collective-permute-done((bf16[2,256,1024]{1,2,0:T(8,128)(2,1)S(1)}, bf16[2,256,1024]{1,2,0:T(8,128)(2,1)S(1)}, u32[]{:S(2)}, u32[]{:S(2)}) %collective-permute-start) | collective-permute-done | bytes 1048608 | tf_op jit(solution)/shard_map/ppermute | solution.py:27
  122.2 1.9 collective-permute-start.1
  124.1 36.2 %collective-permute-done.1 = bf16[2,256,1024]{1,2,0:T(8,128)(2,1)} collective-permute-done((bf16[2,256,1024]{1,2,0:T(8,128)(2,1)S(1)}, bf16[2,256,1024]{1,2,0:T(8,128)(2,1)}, u32[]{:S(2)}, u32[]{:S(2)}) %collective-permute-start.1) | collective-permute-done | bytes 1048608 | tf_op jit(solution)/shard_map/ppermute | solution.py:27
  160.4 1.9 collective-permute-start.2
  162.4 1.0 fusion.58
  163.4 22.4 %collective-permute-done.2 = bf16[2,256,1024]{1,2,0:T(8,128)(2,1)} collective-permute-done((bf16[2,256,1024]{1,2,0:T(8,128)(2,1)}, bf16[2,256,1024]{1,2,0:T(8,128)(2,1)}, u32[]{:S(2)}, u32[]{:S(2)}) %collective-permute-start.2) | collective-permute-done | bytes 1048608 | tf_op jit(solution)/shard_map/ppermute | solution.py:27
  185.8 1.9 collective-permute-start.3
  187.8 12.8 %while.25 = (s32[]{:T(128)}, f32[16,2048]{1,0:T(8,128)S(1)}, s32[]{:T(128)}, f32[16,16,2048]{2,1,0:T(8,128)}, f32[16,16,2048]{2,1,0:T(8,128)}, /*index=5*/s32[]{:T(128)}, s32[]{:T(128)}, s32[]{:T(128)}) while((s32[]{:T(128)}, f32[16,2048]{1,0:T(8,128)S(1)}, s32[]{:T(128)}, f32[16,16,2048]{2,1,0:T(8,128)}, f32[16,16,2048]{2,1,0:T(8,128)}, ...), condition=%wide.region_21.22_spmd, body=%wide.region_20.21_spmd.sunk | while | flops 65541 | bytes 524419 | solution.py:21
  187.8 1.0 bitcast_add_fusion.3
  188.8 1.0 bitcast_add_fusion.3
  189.9 1.0 bitcast_add_fusion.3
  191.0 1.0 bitcast_add_fusion.3
  192.0 1.0 bitcast_add_fusion.3
  193.1 1.0 bitcast_add_fusion.3
  194.1 1.0 bitcast_add_fusion.3
  195.2 1.0 bitcast_add_fusion.3
  196.2 1.0 bitcast_add_fusion.3
  197.3 1.0 bitcast_add_fusion.3
  198.3 1.0 bitcast_add_fusion.3
  199.4 1.0 bitcast_add_fusion.3
  200.7 10.0 %multiply_reduce_fusion.16 = (f32[256]{0:T(256)S(1)}, f32[256,2048]{1,0:T(8,128)S(1)}) fusion(f32[2048]{0:T(1024)S(1)} %bitcast.461, f32[256,2048]{1,0:T(8,128)} %copy-done.2, f32[2048]{0:T(1024)S(1)} %bitcast.459, f32[256]{0:T(256)S(1)} %bitcast.478, f32[2048]{0:T(1024)S(1)} %bitcast.462, f32[2048]{0:T(1024)S(1)} %bitcast.445, f32[256]{0:T(256)S(1)} %bitcast.479, ...), kind=kLoop, calls=%fused_computation.158 | loop fusion | flops 34602752 | bytes 6571008 | tf_op jit(solution)/shard_map/reduce_sum | solution.py:143
  211.3 1.3 constant_dynamic-update-slice_fusion.4
  212.6 1.3 constant_dynamic-update-slice_fusion.3
  213.9 1.3 constant_dynamic-update-slice_fusion.2
  215.7 2.1 fusion.35
  217.8 2.4 %fusion.33 = f32[8,256]{1,0:T(8,128)S(1)} fusion(f32[8,1280,256]{2,1,0:T(8,128)S(1)} %get-tuple-element.324, f32[8,256]{1,0:T(8,128)S(1)} %get-tuple-element.323, pred[256,1280]{0,1:T(8,128)(4,1)S(1)} %fusion.58), kind=kLoop, calls=%fused_computation.134 | loop fusion | flops 10483712 | bytes 10829824 | tf_op jit(solution)/shard_map/reduce_sum | solution.py:51
  220.2 2.8 %divide_convert_fusion = bf16[256,8,128]{0,2,1:T(8,128)(2,1)S(1)} fusion(bf16[1280,8,128]{0,2,1:T(8,128)(2,1)S(1)} %bitcast.366, f32[8,1280,256]{2,1,0:T(8,128)S(1)} %get-tuple-element.324, f32[8,256]{1,0:T(8,128)S(1)} %get-tuple-element.323, pred[256,1280]{0,1:T(8,128)(4,1)S(1)} %fusion.58, f32[256,8]{0,1:T(8,128)S(1)} %bitcast.476), kind=kOutput, calls=%fused_computation.169 | convolution fusion | flops 682098688 | bytes 13975552 | tf_op jit(solution)/shard_map/hqk,khd->qhd/dot_general | solution.py:53
  223.3 0.7 copy.25
  (177 shorter events, 31.4 us)
Async XLA Ops:
  6.5 209.2 %copy-start = (bf16[256,1024]{1,0:T(8,128)(2,1)S(1)}, bf16[256,1024]{1,0:T(8,128)(2,1)}, u32[]{:S(2)}) copy-start(bf16[256,1024]{1,0:T(8,128)(2,1)} %param.15) | copy-start | bytes 1572868
  6.5 181.2 %all-gather.5.cloned.1.call-start = ((), (), s32[]{:S(2)}) async-start(), calls=%async_computation | async-start | bytes 2228224 | tf_op jit(solution)/shard_map/all_gather | solution.py:13
  10.8 2.6 %copy-start.7 = (f32[16,2048]{1,0:T(8,128)S(1)}, f32[16,2048]{1,0:T(8,128)}, u32[]{:S(2)}) copy-start(f32[16,2048]{1,0:T(8,128)} %param.22) | copy-start | bytes 393220
  10.8 3.4 %copy-start.8 = (f32[2,16,256]{2,1,0:T(8,128)S(1)}, f32[2,16,256]{2,1,0:T(8,128)}, u32[]{:S(2)}) copy-start(f32[2,16,256]{2,1,0:T(8,128)} %param.23) | copy-start | bytes 98308
  12.1 1.4 copy-start.2
  14.1 173.6 %all-gather.7.cloned.1.call-start = ((), (), s32[]{:S(2)}) async-start(), calls=%async_computation.1 | async-start | bytes 2228224 | tf_op jit(solution)/shard_map/all_gather | solution.py:13
  14.2 0.6 copy-start.5
  83.8 0.7 copy-start.1
  84.5 39.6 %copy-start.6 = (f32[256,16]{0,1:T(8,128)S(1)}, f32[256,16]{0,1:T(8,128)}, u32[]{:S(2)}) copy-start(f32[256,16]{0,1:T(8,128)} %copy-done.5) | copy-start | bytes 49156
  87.1 35.1 %collective-permute-start = (bf16[2,256,1024]{1,2,0:T(8,128)(2,1)S(1)}, bf16[2,256,1024]{1,2,0:T(8,128)(2,1)S(1)}, u32[]{:S(2)}, u32[]{:S(2)}) collective-permute-start(bf16[2,256,1024]{1,2,0:T(8,128)(2,1)S(1)} %pad_maximum_fusion), channel_id=1, source_target_pairs={{0,2},{2,4},{4,6},{6,8},{8,10},{10,12},{12,14},{14,16},{16,18},{18... | collective-permute-start | bytes 3145736 | tf_op jit(solution)/shard_map/ppermute | solution.py:27
  122.2 38.2 %collective-permute-start.1 = (bf16[2,256,1024]{1,2,0:T(8,128)(2,1)S(1)}, bf16[2,256,1024]{1,2,0:T(8,128)(2,1)}, u32[]{:S(2)}, u32[]{:S(2)}) collective-permute-start(bf16[2,256,1024]{1,2,0:T(8,128)(2,1)S(1)} %collective-permute-done), channel_id=1, source_target_pairs={{0,2},{2,4},{4,6},{6,8},{8,10},{10,12},{12,14},{14,16},{16,18},{18... | collective-permute-start | bytes 3145736 | tf_op jit(solution)/shard_map/ppermute | solution.py:27
  160.4 25.4 %collective-permute-start.2 = (bf16[2,256,1024]{1,2,0:T(8,128)(2,1)}, bf16[2,256,1024]{1,2,0:T(8,128)(2,1)}, u32[]{:S(2)}, u32[]{:S(2)}) collective-permute-start(bf16[2,256,1024]{1,2,0:T(8,128)(2,1)} %collective-permute-done.1), channel_id=1, source_target_pairs={{0,2},{2,4},{4,6},{6,8},{8,10},{10,12},{12,14},{14,16},{16,18},{18... | collective-permute-start | bytes 3145736 | tf_op jit(solution)/shard_map/ppermute | solution.py:27
  185.8 25.6 %collective-permute-start.3 = (bf16[2,256,1024]{1,2,0:T(8,128)(2,1)}, bf16[2,256,1024]{1,2,0:T(8,128)(2,1)}, u32[]{:S(2)}, u32[]{:S(2)}) collective-permute-start(bf16[2,256,1024]{1,2,0:T(8,128)(2,1)} %collective-permute-done.2), channel_id=1, source_target_pairs={{0,2},{2,4},{4,6},{6,8},{8,10},{10,12},{12,14},{14,16},{16,18},{18... | collective-permute-start | bytes 3145736 | tf_op jit(solution)/shard_map/ppermute | solution.py:27
  200.7 10.0 %copy-start.3 = (bf16[2048,128]{1,0:T(8,128)(2,1)S(1)}, bf16[2048,128]{1,0:T(8,128)(2,1)}, u32[]{:S(2)}) copy-start(bf16[2048,128]{1,0:T(8,128)(2,1)} %param.25) | copy-start | bytes 1572868
  220.2 2.8 %copy-start.4 = (bf16[1024,128]{1,0:T(8,128)(2,1)S(1)}, bf16[1024,128]{1,0:T(8,128)(2,1)}, u32[]{:S(2)}) copy-start(bf16[1024,128]{1,0:T(8,128)(2,1)} %param.24) | copy-start | bytes 786436
Sparse Core Ops, SparseCore 0:
  14.3 60.3 all-gather.4
  84.6 71.3 all-gather.6
where the time goes:
time: 233 us; the launch traced here: 231 us
  waiting for transfers between devices  90.4 us (39%)
  local copies, waits for them, and re-layouts  57.2 us (25%)
  other arithmetic  48.1 us (21%)
  between operations  13.7 us (6%)
  matrix products  11.2 us (5%)
  starting transfers between devices  9.19 us (4%)
    ppermute x4, waiting for transfers between devices, from_behind(): lax.ppermute(value, axis, [(source, source + steps) for source in range(i...  90.3 us
    slice x16, local copies, waits for them, and re-layouts, advance(): inflow_blk[offset][None, :]  31.9 us
    reduce_sum x80, other arithmetic, advance(): collected.append(jnp.sum(out_blk[offset][:, None] * running, 0))  21.4 us
    add x12, other arithmetic, combine(): return (earlier[0] * following[0], following[0] * earlier[1] + following[1])  12.4 us
    dynamic_update_slice x16, local copies, waits for them, and re-layouts, run_mixer(): lax.scan(advance, carry_state, (timestep.reshape(groups, block_len, -1),...  10.6 us
    reduce_sum x1, other arithmetic, per_device(): jnp.mean(outputs * outputs, -1, keepdims=True) + 1e-05  10 us
    ppermute x4, starting transfers between devices, from_behind(): lax.ppermute(value, axis, [(source, source + steps) for source in range(i...  9.15 us
    unnamed x24, local copies, waits for them, and re-layouts  8.86 us
  transfers between devices with their start and end apart: 6, of which 3 were waited for; matrix products, arithmetic and copies ran while one was open for 41% of the time, Pallas kernels for 0%

commit v1 on v0

v1 whole, which is shorter than its diff:
```python
import functools
import math

import jax
import jax.numpy as jnp
from jax import lax
from jax.experimental import pallas as pl
from jax.experimental.pallas import tpu as pltpu
from jax.sharding import PartitionSpec as P

HD = 128
LANES = 128
GROUP = 4
LOG2E = math.log2(math.e)


def nt_dot(a, b):
    return lax.dot_general(a, b, (((1,), (1,)), ((), ())), preferred_element_type=jnp.float32)


def block_kernel(
    n,
    q_hbm,
    k_hbm,
    v_hbm,
    ch_ref,
    low_ref,
    proj_ref,
    bias_ref,
    dlog_ref,
    maps_ref,
    aw_ref,
    mw_ref,
    out_ref,
    qb,
    kb,
    vb,
    pk,
    pv,
    att,
    stage,
    dts,
    us,
    decays,
    rate,
    msg_out,
    msg_in,
    local_sem,
    plane_send,
    plane_recv,
    next_send,
    next_recv,
    state_send,
    state_recv,
    att_send,
    att_recv,
):
    rows, feats = q_hbm.shape
    width = feats // GROUP
    heads_here = width // HD
    ns = dlog_ref.shape[0]
    cb = dlog_ref.shape[1] // LANES
    state_rows = ns * cb
    me = lax.axis_index("ctx")
    group = lax.div(me, GROUP)
    place = lax.rem(me, GROUP)
    base = group * GROUP
    hops = []
    while 2 ** len(hops) < n:
        hops.append(2 ** len(hops))

    barrier = pltpu.get_barrier_semaphore()
    greeted = 0
    for r in range(1, GROUP):
        pl.semaphore_signal(barrier, inc=1, device_id={"ctx": base + lax.rem(place + r, GROUP)})
        greeted += 1
    for d in hops:
        pl.semaphore_signal(barrier, inc=1, device_id={"ctx": lax.rem(me + d, n)})
        pl.semaphore_signal(barrier, inc=1, device_id={"ctx": lax.rem(me + n - d, n)})
        greeted += 2
    pl.semaphore_wait(barrier, greeted)

    def columns(where):
        return pl.ds(pl.multiple_of(where * width, LANES), width)

    def block(where):
        return pl.ds(pl.multiple_of(where * rows, rows), rows)

    pairs = ((k_hbm, kb, pk), (v_hbm, vb, pv), (q_hbm, qb, None))

    def plane_copy(a, r):
        there = lax.rem(place + r, GROUP)
        source, buffer, _ = pairs[a]
        return pltpu.make_async_remote_copy(
            src_ref=source.at[:, columns(there)],
            dst_ref=buffer.at[block(place), :],
            send_sem=plane_send.at[a, r],
            recv_sem=plane_recv.at[a, r],
            device_id={"ctx": base + there},
        )

    def own_copy(a):
        source, buffer, _ = pairs[a]
        return pltpu.make_async_copy(
            source.at[:, columns(place)], buffer.at[block(place), :], local_sem.at[a]
        )

    def next_copy(a, r):
        source, buffer, far = pairs[a]
        which = lax.rem(place + GROUP - r, GROUP)
        return pltpu.make_async_remote_copy(
            src_ref=source.at[:, columns(place)] if r == 0 else buffer.at[block(which), :],
            dst_ref=far.at[block(which), :],
            send_sem=next_send.at[a, r],
            recv_sem=next_recv.at[a, r],
            device_id={"ctx": lax.rem(me + GROUP, n)},
        )

    has_next = me + GROUP < n
    has_before = group > 0

    for a in range(2):
        for r in range(1, GROUP):
            plane_copy(a, r).start()
    if n > GROUP:

        @pl.when(has_next)
        def _():
            for a in range(2):
                next_copy(a, 0).start()

    for a in range(3):
        own_copy(a).start()

    for j in range(cb):
        cols = slice(j * LANES, (j + 1) * LANES)
        rate[pl.ds(j, ns, stride=cb), :] = -jnp.exp(dlog_ref[:, cols]) * LOG2E
    for j in range(cb):
        cols = slice(j * LANES, (j + 1) * LANES)
        raw = jnp.dot(low_ref[...], proj_ref[:, cols], preferred_element_type=jnp.float32)
        raw = raw + bias_ref[:, cols]
        step = jnp.maximum(raw, 0.0) + jnp.log1p(jnp.exp(-jnp.abs(raw)))
        dts[pl.ds(j, rows, stride=cb), :] = step
        us[pl.ds(j, rows, stride=cb), :] = step * ch_ref[:, cols].astype(jnp.float32)

    def first_pass(t, carry):
        total, state = carry[0], carry[1:]
        here = pl.ds(pl.multiple_of(t * cb, cb), cb)
        step = dts[here, :]
        flow = us[here, :]
        new = []
        for s in range(ns):
            decay = jnp.exp2(step * rate[s * cb : (s + 1) * cb, :])
            decays[pl.ds(pl.multiple_of(t * state_rows, cb) + s * cb, cb), :] = decay
            new.append(decay * state[s] + maps_ref[0, s, t] * flow)
        return (total + step, *new)

    zero = jnp.zeros((cb, LANES), jnp.float32)
    carry = (zero,) * (ns + 1)

    def forward(r):
        for a in range(2):
            plane_copy(a, r).wait_recv()

        @pl.when(has_next)
        def _():
            for a in range(2):
                next_copy(a, r).start()

    cuts = [0, rows // 2, 3 * rows // 4, rows]
    for r in range(1, GROUP):
        carry = lax.fori_loop(cuts[r - 1], cuts[r], first_pass, carry)
        if n > GROUP:
            forward(r)
        else:
            for a in range(2):
                plane_copy(a, r).wait_recv()

    def state_copy(k, d):
        return pltpu.make_async_remote_copy(
            src_ref=msg_out.at[k],
            dst_ref=msg_in.at[k],
            send_sem=state_send.at[k],
            recv_sem=state_recv.at[k],
            device_id={"ctx": lax.rem(me + d, n)},
        )

    def spread(total):
        return jnp.concatenate([total] * ns, 0)

    held = jnp.concatenate(carry[1:], 0)
    total = carry[0]
    msg_out[0, :state_rows, :] = held
    msg_out[0, state_rows:, :] = total
    before = msg_out.at[len(hops)]
    before[...] = jnp.zeros_like(before)
    for k, d in enumerate(hops):

        @pl.when(me + d < n)
        def _():
            state_copy(k, d).start()

        if k == 0:
            for r in range(1, GROUP):
                plane_copy(2, r).start()
        last = k + 1 == len(hops)
        if not last:
            msg_out[k + 1] = msg_out[k]

        @pl.when(me >= d)
        def _():
            state_copy(k, d).wait_recv()
            arrived = msg_in[k, :state_rows, :]
            arrived_total = msg_in[k, state_rows:, :]
            spans = before[state_rows:, :]
            before[:state_rows, :] = (
                jnp.exp2(rate[...] * spread(spans)) * arrived + before[:state_rows, :]
            )
            before[state_rows:, :] = spans + arrived_total
            if not last:
                spans = msg_out[k, state_rows:, :]
                msg_out[k + 1, :state_rows, :] = (
                    jnp.exp2(rate[...] * spread(spans)) * arrived + msg_out[k, :state_rows, :]
                )
                msg_out[k + 1, state_rows:, :] = spans + arrived_total

    def second_pass(t, state):
        here = pl.ds(pl.multiple_of(t * cb, cb), cb)
        flow = us[here, :]
        new = []
        out = None
        for s in range(ns):
            decay = decays[pl.ds(pl.multiple_of(t * state_rows, cb) + s * cb, cb), :]
            value = decay * state[s] + maps_ref[0, s, t] * flow
            new.append(value)
            term = maps_ref[1, s, t] * value
            out = term if out is None else out + term
        dts[here, :] = out
        return tuple(new)

    lax.fori_loop(
        0,
        rows,
        second_pass,
        tuple(before[s * cb : (s + 1) * cb, :] for s in range(ns)),
    )

    squares = jnp.zeros((rows, LANES), jnp.float32)
    for j in range(cb):
        part = dts[pl.ds(j, rows, stride=cb), :]
        squares = squares + part * part
    scale = lax.rsqrt(jnp.sum(squares, -1, keepdims=True) / (cb * LANES) + 1e-05)
    combined = jnp.zeros((rows, out_ref.shape[1]), jnp.float32)
    for j in range(cb):
        part = (dts[pl.ds(j, rows, stride=cb), :] * scale).astype(jnp.bfloat16)
        combined = combined + jnp.dot(
            part, mw_ref[j * LANES : (j + 1) * LANES, :], preferred_element_type=jnp.float32
        )

    for a in range(3):
        own_copy(a).wait()
    for r in range(1, GROUP):
        plane_copy(2, r).wait_recv()
    if n > GROUP:

        @pl.when(has_before)
        def _():
            for r in range(GROUP):
                for a in range(2):
                    next_copy(a, r).wait_recv()

    @pl.when(group == 0)
    def _():
        pk[...] = jnp.zeros_like(pk)
        pv[...] = jnp.zeros_like(pv)

    def att_copy(s):
        return pltpu.make_async_remote_copy(
            src_ref=stage.at[s],
            dst_ref=att.at[place],
            send_sem=att_send.at[s],
            recv_sem=att_recv.at[place],
            device_id={"ctx": base + s},
        )

    shut = jnp.where(has_before, 0, GROUP * rows).astype(jnp.int32)
    for s in range(GROUP):
        near = (s + 1) * rows
        far = (GROUP - s) * rows
        near_open = lax.broadcasted_iota(jnp.int32, (rows, near), 1) <= (
            lax.broadcasted_iota(jnp.int32, (rows, near), 0) + s * rows
        )
        far_open = lax.broadcasted_iota(jnp.int32, (rows, far), 1) > (
            lax.broadcasted_iota(jnp.int32, (rows, far), 0) + shut
        )
        for h in range(heads_here):
            cols = slice(h * HD, (h + 1) * HD)
            query = qb[s * rows : (s + 1) * rows, cols]
            factor = LOG2E / math.sqrt(HD)
            near_scores = nt_dot(query, kb[:near, cols]) * factor
            far_scores = nt_dot(query, pk[s * rows :, cols]) * factor
            near_scores = jnp.where(near_open, near_scores, -1e30)
            far_scores = jnp.where(far_open, far_scores, -1e30)
            top = jnp.maximum(
                jnp.max(near_scores, -1, keepdims=True), jnp.max(far_scores, -1, keepdims=True)
            )
            near_terms = jnp.exp2(near_scores - top)
            far_terms = jnp.exp2(far_scores - top)
            row_sum = jnp.sum(near_terms, -1, keepdims=True) + jnp.sum(
                far_terms, -1, keepdims=True
            )
            summed = jnp.dot(
                near_terms.astype(jnp.bfloat16), vb[:near, cols], preferred_element_type=jnp.float32
            ) + jnp.dot(
                far_terms.astype(jnp.bfloat16),
                pv[s * rows :, cols],
                preferred_element_type=jnp.float32,
            )
            stage[s, :, cols] = (summed / row_sum).astype(jnp.bfloat16)

        @pl.when(place != s)
        def _():
            att_copy(s).start()

    for s in range(GROUP):

        @pl.when(place != s)
        def _():
            pltpu.make_async_remote_copy(
                src_ref=stage.at[s],
                dst_ref=att.at[s],
                send_sem=att_send.at[s],
                recv_sem=att_recv.at[s],
                device_id={"ctx": base + s},
            ).wait_recv()

        @pl.when(place == s)
        def _():
            att[s] = stage[s]

    for s in range(GROUP):
        combined = combined + jnp.dot(
            att[s], aw_ref[s * width : (s + 1) * width, :], preferred_element_type=jnp.float32
        )
    mean = jnp.mean(combined * combined, -1, keepdims=True)
    out_ref[...] = (combined * lax.rsqrt(mean + 1e-06)).astype(out_ref.dtype)

    for a in range(3):
        for r in range(1, GROUP):
            plane_copy(a, r).wait_send()
    if n > GROUP:

        @pl.when(has_next)
        def _():
            for r in range(GROUP):
                for a in range(2):
                    next_copy(a, r).wait_send()

    for k, d in enumerate(hops):

        @pl.when(me + d < n)
        def _():
            state_copy(k, d).wait_send()

    for s in range(GROUP):

        @pl.when(place != s)
        def _():
            att_copy(s).wait_send()


def per_device(
    n,
    query_rows,
    key_rows,
    value_rows,
    channels,
    step_low,
    step_proj,
    step_bias,
    decay_log,
    state_maps,
    attend_weight,
    mixer_weight,
):
    rows, feats = query_rows.shape
    width = feats // GROUP
    ns, ch = decay_log.shape
    cb = ch // LANES
    rounds = max(1, (n - 1).bit_length())
    any_spec = pl.BlockSpec(memory_space=pl.ANY)
    vmem = pl.BlockSpec(memory_space=pltpu.VMEM)
    smem = pl.BlockSpec(memory_space=pltpu.SMEM)
    wide = pltpu.VMEM((GROUP * rows, width), jnp.bfloat16)
    dma = pltpu.SemaphoreType.DMA
    return pl.pallas_call(
        functools.partial(block_kernel, n),
        out_shape=jax.ShapeDtypeStruct((rows, attend_weight.shape[1]), jnp.bfloat16),
        in_specs=[any_spec] * 3 + [vmem] * 5 + [smem] + [vmem] * 2,
        out_specs=vmem,
        scratch_shapes=[
            wide,
            wide,
            wide,
            wide,
            wide,
            pltpu.VMEM((GROUP, rows, width), jnp.bfloat16),
            pltpu.VMEM((GROUP, rows, width), jnp.bfloat16),
            pltpu.VMEM((rows * cb, LANES), jnp.float32),
            pltpu.VMEM((rows * cb, LANES), jnp.float32),
            pltpu.VMEM((rows * ns * cb, LANES), jnp.float32),
            pltpu.VMEM((ns * cb, LANES), jnp.float32),
            pltpu.VMEM((rounds + 1, (ns + 1) * cb, LANES), jnp.float32),
            pltpu.VMEM((rounds, (ns + 1) * cb, LANES), jnp.float32),
            dma((3,)),
            dma((3, GROUP)),
            dma((3, GROUP)),
            dma((2, GROUP)),
            dma((2, GROUP)),
            dma((rounds,)),
            dma((rounds,)),
            dma((GROUP,)),
            dma((GROUP,)),
        ],
        compiler_params=pltpu.CompilerParams(
            collective_id=0, has_side_effects=True, vmem_limit_bytes=60 * 1024 * 1024
        ),
    )(
        query_rows,
        key_rows,
        value_rows,
        channels,
        step_low,
        step_proj,
        step_bias.reshape(1, -1),
        decay_log,
        state_maps,
        attend_weight,
        mixer_weight,
    )


def solution(mesh):
    return jax.shard_map(
        functools.partial(per_device, mesh.shape["ctx"]),
        mesh=mesh,
        in_specs=(
            P(("dp", "ctx"), None),
            P(("dp", "ctx"), None),
            P(("dp", "ctx"), None),
            P(("dp", "ctx"), None),
            P(("dp", "ctx"), None),
            P(),
            P(),
            P(),
            P(None, None, ("dp", "ctx")),
            P(),
            P(),
        ),
        out_specs=P(("dp", "ctx"), None),
        check_vma=False,
    )
```

time: 233 us -> 73.4 us (0.32)
  the two profiles are of different devices: /device:TPU:24 before, /device:TPU:30 now
where the time goes in v1:
time: 73.4 us; the launch traced here: 73.2 us
  Pallas kernels  71.7 us (98%)
  local copies, waits for them, and re-layouts  1.47 us (2%)
    pallas_call x1, Pallas kernels, per_device(): pl.pallas_call(functools.partial(block_kernel, n), out_shape=jax.ShapeDty...  71.7 us
    unnamed x1, local copies, waits for them, and re-layouts  1.47 us

profile of v1, /device:TPU:30, one launch (start us, length us, event | category | flops | bytes accessed | tf_op | source)
XLA Modules:
  0.0 73.2 jit_solution(16668401842696590239)
XLA Ops:
  0.0 71.7 %shard_map.109 = bf16[256,128]{1,0:T(8,128)(2,1)} custom-call(bf16[256,1024]{1,0:T(8,128)(2,1)} %q_hbm.1, bf16[256,1024]{1,0:T(8,128)(2,1)} %k_hbm.1, bf16[256,1024]{1,0:T(8,128)(2,1)} %v_hbm.1, bf16[256,2048]{1,0:T(8,128)(2,1)} %ch_ref.1, bf16[256,128]{1,0:T(8,128)(2,1)} %low_ref.1, bf16[128,2048]{1,0:T(8,128)(2,1)} %proj_ref.1, f32[1,2048]{1,0:T(1,128)} %bitcast.1, ...), custom_call_target="tpu_custom_call" | custom-call | tf_op jit(solution)/shard_map/pallas_call | solution.py:396
  71.7 1.5 %copy.13 = bf16[256,128]{1,0:T(8,128)(2,1)} copy(bf16[256,128]{1,0:T(8,128)(2,1)} %shard_map.109) | data formatting | bytes 131072

commit v2 on v1

--- a/solution.py
+++ b/solution.py
@@ -43,15 +43,23 @@
     us,
     decays,
     rate,
-    msg_out,
-    msg_in,
+    quarter_out,
+    quarter_in,
+    far_out,
+    far_in,
+    enter_out,
+    enter,
     local_sem,
     plane_send,
     plane_recv,
     next_send,
     next_recv,
-    state_send,
-    state_recv,
+    quarter_send,
+    quarter_recv,
+    far_send,
+    far_recv,
+    enter_send,
+    enter_recv,
     att_send,
     att_recv,
 ):
@@ -66,8 +74,8 @@
     place = lax.rem(me, GROUP)
     base = group * GROUP
     hops = []
-    while 2 ** len(hops) < n:
-        hops.append(2 ** len(hops))
+    while GROUP * 2 ** len(hops) < n:
+        hops.append(GROUP * 2 ** len(hops))
 
     barrier = pltpu.get_barrier_semaphore()
     greeted = 0
@@ -131,6 +139,8 @@
 
     for a in range(3):
         own_copy(a).start()
+    for r in range(1, GROUP):
+        plane_copy(2, r).start()
 
     for j in range(cb):
         cols = slice(j * LANES, (j + 1) * LANES)
@@ -169,93 +179,102 @@
 
     cuts = [0, rows // 2, 3 * rows // 4, rows]
     for r in range(1, GROUP):
-        carry = lax.fori_loop(cuts[r - 1], cuts[r], first_pass, carry)
+        carry = lax.fori_loop(cuts[r - 1], cuts[r], first_pass, carry, unroll=2)
         if n > GROUP:
             forward(r)
         else:
             for a in range(2):
                 plane_copy(a, r).wait_recv()
 
-    def state_copy(k, d):
+    part = state_rows // GROUP
+    mine = pl.ds(pl.multiple_of(place * part, part), part)
+
+    def quarter_copy(r):
+        there = lax.rem(place + r, GROUP)
         return pltpu.make_async_remote_copy(
-            src_ref=msg_out.at[k],
-            dst_ref=msg_in.at[k],
-            send_sem=state_send.at[k],
-            recv_sem=state_recv.at[k],
+            src_ref=quarter_out.at[there],
+            dst_ref=quarter_in.at[place],
+            send_sem=quarter_send.at[r],
+            recv_sem=quarter_recv.at[r],
+            device_id={"ctx": base + there},
+        )
+
+    def far_copy(k, d):
+        return pltpu.make_async_remote_copy(
+            src_ref=far_out.at[k],
+            dst_ref=far_in.at[k],
+            send_sem=far_send.at[k],
+            recv_sem=far_recv.at[k],
             device_id={"ctx": lax.rem(me + d, n)},
         )
 
-    def spread(total):
-        return jnp.concatenate([total] * ns, 0)
-
-    held = jnp.concatenate(carry[1:], 0)
-    total = carry[0]
-    msg_out[0, :state_rows, :] = held
-    msg_out[0, state_rows:, :] = total
-    before = msg_out.at[len(hops)]
+    def enter_copy(r):
+        there = lax.rem(place + r, GROUP)
+        return pltpu.make_async_remote_copy(
+            src_ref=enter_out.at[there],
+            dst_ref=enter.at[mine, :],
+            send_sem=enter_send.at[r],
+            recv_sem=enter_recv.at[r],
+            device_id={"ctx": base + there},
+        )
+
+    def through(spans):
+        return jnp.exp2(rate[mine, :] * jnp.concatenate([spans] * (part // cb), 0))
+
+    states_each = part // cb
+    for q in range(GROUP):
+        for i in range(states_each):
+            quarter_out[q, i * cb : (i + 1) * cb, :] = carry[1 + q * states_each + i]
+        quarter_out[q, part:, :] = carry[0]
+    for r in range(1, GROUP):
+        quarter_copy(r).start()
+    quarter_in[place] = quarter_out[place]
+    for r in range(1, GROUP):
+        quarter_copy(r).wait_recv()
+
+    run_state = jnp.zeros((part, LANES), jnp.float32)
+    run_total = jnp.zeros((cb, LANES), jnp.float32)
+    entries = []
+    for q in range(GROUP):
+        entries.append((run_state, run_total))
+        spans = quarter_in[q, part:, :]
+        run_state = through(spans) * run_state + quarter_in[q, :part, :]
+        run_total = run_total + spans
+
+    before = far_out.at[len(hops)]
     before[...] = jnp.zeros_like(before)
+    if hops:
+        far_out[0, :part, :] = run_state
+        far_out[0, part:, :] = run_total
     for k, d in enumerate(hops):
 
         @pl.when(me + d < n)
         def _():
-            state_copy(k, d).start()
-
-        if k == 0:
-            for r in range(1, GROUP):
-                plane_copy(2, r).start()
+            far_copy(k, d).start()
+
         last = k + 1 == len(hops)
         if not last:
-            msg_out[k + 1] = msg_out[k]
+            far_out[k + 1] = far_out[k]
 
         @pl.when(me >= d)
         def _():
-            state_copy(k, d).wait_recv()
-            arrived = msg_in[k, :state_rows, :]
-            arrived_total = msg_in[k, state_rows:, :]
-            spans = before[state_rows:, :]
-            before[:state_rows, :] = (
-                jnp.exp2(rate[...] * spread(spans)) * arrived + before[:state_rows, :]
-            )
-            before[state_rows:, :] = spans + arrived_total
+            far_copy(k, d).wait_recv()
+            arrived = far_in[k, :part, :]
+            arrived_total = far_in[k, part:, :]
+            spans = before[part:, :]
+            before[:part, :] = through(spans) * arrived + before[:part, :]
+            before[part:, :] = spans + arrived_total
             if not last:
-                spans = msg_out[k, state_rows:, :]
-                msg_out[k + 1, :state_rows, :] = (
-                    jnp.exp2(rate[...] * spread(spans)) * arrived + msg_out[k, :state_rows, :]
-                )
-                msg_out[k + 1, state_rows:, :] = spans + arrived_total
-
-    def second_pass(t, state):
-        here = pl.ds(pl.multiple_of(t * cb, cb), cb)
-        flow = us[here, :]
-        new = []
-        out = None
-        for s in range(ns):
-            decay = decays[pl.ds(pl.multiple_of(t * state_rows, cb) + s * cb, cb), :]
-            value = decay * state[s] + maps_ref[0, s, t] * flow
-            new.append(value)
-            term = maps_ref[1, s, t] * value
-            out = term if out is None else out + term
-        dts[here, :] = out
-        return tuple(new)
-
-    lax.fori_loop(
-        0,
-        rows,
-        second_pass,
-        tuple(before[s * cb : (s + 1) * cb, :] for s in range(ns)),
-    )
-
-    squares = jnp.zeros((rows, LANES), jnp.float32)
-    for j in range(cb):
-        part = dts[pl.ds(j, rows, stride=cb), :]
-        squares = squares + part * part
-    scale = lax.rsqrt(jnp.sum(squares, -1, keepdims=True) / (cb * LANES) + 1e-05)
-    combined = jnp.zeros((rows, out_ref.shape[1]), jnp.float32)
-    for j in range(cb):
-        part = (dts[pl.ds(j, rows, stride=cb), :] * scale).astype(jnp.bfloat16)
-        combined = combined + jnp.dot(
-            part, mw_ref[j * LANES : (j + 1) * LANES, :], preferred_element_type=jnp.float32
-        )
+                spans = far_out[k, part:, :]
+                far_out[k + 1, :part, :] = through(spans) * arrived + far_out[k, :part, :]
+                far_out[k + 1, part:, :] = spans + arrived_total
+
+    group_state = before[:part, :]
+    for q in range(GROUP):
+        enter_out[q] = through(entries[q][1]) * group_state + entries[q][0]
+    for r in range(1, GROUP):
+        enter_copy(r).start()
+    enter[mine, :] = enter_out[place]
 
     for a in range(3):
         own_copy(a).wait()
@@ -322,6 +341,42 @@
         def _():
             att_copy(s).start()
 
+    def second_pass(t, state):
+        here = pl.ds(pl.multiple_of(t * cb, cb), cb)
+        flow = us[here, :]
+        new = []
+        out = None
+        for s in range(ns):
+            decay = decays[pl.ds(pl.multiple_of(t * state_rows, cb) + s * cb, cb), :]
+            value = decay * state[s] + maps_ref[0, s, t] * flow
+            new.append(value)
+            term = maps_ref[1, s, t] * value
+            out = term if out is None else out + term
+        dts[here, :] = out
+        return tuple(new)
+
+    for r in range(1, GROUP):
+        enter_copy(r).wait_recv()
+    lax.fori_loop(
+        0,
+        rows,
+        second_pass,
+        tuple(enter[s * cb : (s + 1) * cb, :] for s in range(ns)),
+        unroll=2,
+    )
+
+    squares = jnp.zeros((rows, LANES), jnp.float32)
+    for j in range(cb):
+        part = dts[pl.ds(j, rows, stride=cb), :]
+        squares = squares + part * part
+    scale = lax.rsqrt(jnp.sum(squares, -1, keepdims=True) / (cb * LANES) + 1e-05)
+    combined = jnp.zeros((rows, out_ref.shape[1]), jnp.float32)
+    for j in range(cb):
+        part = (dts[pl.ds(j, rows, stride=cb), :] * scale).astype(jnp.bfloat16)
+        combined = combined + jnp.dot(
+            part, mw_ref[j * LANES : (j + 1) * LANES, :], preferred_element_type=jnp.float32
+        )
+
     for s in range(GROUP):
 
         @pl.when(place != s)
@@ -356,11 +411,14 @@
                 for a in range(2):
                     next_copy(a, r).wait_send()
 
+    for r in range(1, GROUP):
+        quarter_copy(r).wait_send()
+        enter_copy(r).wait_send()
     for k, d in enumerate(hops):
 
         @pl.when(me + d < n)
         def _():
-            state_copy(k, d).wait_send()
+            far_copy(k, d).wait_send()
 
     for s in range(GROUP):
 
@@ -387,7 +445,8 @@
     width = feats // GROUP
     ns, ch = decay_log.shape
     cb = ch // LANES
-    rounds = max(1, (n - 1).bit_length())
+    rounds = max(1, (n // GROUP - 1).bit_length())
+    part = ns * cb // GROUP
     any_spec = pl.BlockSpec(memory_space=pl.ANY)
     vmem = pl.BlockSpec(memory_space=pltpu.VMEM)
     smem = pl.BlockSpec(memory_space=pltpu.SMEM)
@@ -410,15 +469,23 @@
             pltpu.VMEM((rows * cb, LANES), jnp.float32),
             pltpu.VMEM((rows * ns * cb, LANES), jnp.float32),
             pltpu.VMEM((ns * cb, LANES), jnp.float32),
-            pltpu.VMEM((rounds + 1, (ns + 1) * cb, LANES), jnp.float32),
-            pltpu.VMEM((rounds, (ns + 1) * cb, LANES), jnp.float32),
+            pltpu.VMEM((GROUP, part + cb, LANES), jnp.float32),
+            pltpu.VMEM((GROUP, part + cb, LANES), jnp.float32),
+            pltpu.VMEM((rounds + 1, part + cb, LANES), jnp.float32),
+            pltpu.VMEM((rounds, part + cb, LANES), jnp.float32),
+            pltpu.VMEM((GROUP, part, LANES), jnp.float32),
+            pltpu.VMEM((ns * cb, LANES), jnp.float32),
             dma((3,)),
             dma((3, GROUP)),
             dma((3, GROUP)),
             dma((2, GROUP)),
             dma((2, GROUP)),
+            dma((GROUP,)),
+            dma((GROUP,)),
             dma((rounds,)),
             dma((rounds,)),
+            dma((GROUP,)),
+            dma((GROUP,)),
             dma((GROUP,)),
             dma((GROUP,)),
         ],

time: 73.4 us -> 57.1 us (0.78)
  the two profiles are of different devices: /device:TPU:30 before, /device:TPU:24 now
where the time goes in v2:
time: 57.1 us; the launch traced here: 56.9 us
  Pallas kernels  55.4 us (97%)
  local copies, waits for them, and re-layouts  1.47 us (3%)
    pallas_call x1, Pallas kernels, per_device(): pl.pallas_call(functools.partial(block_kernel, n), out_shape=jax.ShapeDty...  55.4 us
    unnamed x1, local copies, waits for them, and re-layouts  1.47 us

profile of v2, /device:TPU:24, one launch (start us, length us, event | category | flops | bytes accessed | tf_op | source)
XLA Modules:
  0.0 56.9 jit_solution(16172239078732326481)
XLA Ops:
  0.0 55.4 %shard_map.109 = bf16[256,128]{1,0:T(8,128)(2,1)} custom-call(bf16[256,1024]{1,0:T(8,128)(2,1)} %q_hbm.1, bf16[256,1024]{1,0:T(8,128)(2,1)} %k_hbm.1, bf16[256,1024]{1,0:T(8,128)(2,1)} %v_hbm.1, bf16[256,2048]{1,0:T(8,128)(2,1)} %ch_ref.1, bf16[256,128]{1,0:T(8,128)(2,1)} %low_ref.1, bf16[128,2048]{1,0:T(8,128)(2,1)} %proj_ref.1, f32[1,2048]{1,0:T(1,128)} %bitcast.1, ...), custom_call_target="tpu_custom_call" | custom-call | tf_op jit(solution)/shard_map/pallas_call | solution.py:455
  55.4 1.5 %copy.13 = bf16[256,128]{1,0:T(8,128)(2,1)} copy(bf16[256,128]{1,0:T(8,128)(2,1)} %shard_map.109) | data formatting | bytes 131072
